TPU v7x, 32 devices: a whole 2x2x4 slice. The times are simulated.
32 devices in a mesh: groups: 2 (over x), mix: 16 (over z, y, core).
Axes of the slice: x: 2, y: 2, z: 4, core: 2. Of those that a mesh axis runs over, the one named last changes fastest.
Arguments:
- resid_in: bfloat16 [4096, 2048], P(('groups', 'mix')), parts along dimension 0, may hold values from -40 to 40
- head_in: bfloat16 [4096, 4096], P('groups', 'mix'), parts along dimension 0, may hold values from -6 to 6
- gate_in: bfloat16 [4096, 4096], P('groups', 'mix'), parts along dimension 0, may hold values from -64 to 64
- in_basis: bfloat16 [4096, 128], P('groups'), parts along dimension 0, may hold values from -6 to 6
- out_basis: bfloat16 [4096, 128], P('groups'), parts along dimension 0, may hold values from -6 to 6
- step_size: float32 [64, 4096], P('mix', 'groups'), parts along dimension 1, may hold values from 0 to 2
- decay_rate: float32 [64], P('mix'), may hold values from 0.5 to 2
- init_state: float32 [16, 64, 64, 128], P('groups', 'mix'), parts along dimension 0, may hold values from -0.6 to 0.6
- lengths: int32 [16], P('groups'), parts along dimension 0, may hold values from 1 to 512, 2048 in all
- norm_gain: float32 [4096], replicated, may hold values from 0.1 to 1.9
- out_proj: bfloat16 [4096, 2048], P('mix'), may hold values from -0.09375 to 0.09375
- moe_gain: float32 [2048], replicated, may hold values from 0.1 to 1.9
- expert_ids: int32 [4096, 8], P(('groups', 'mix')), parts along dimension 0, may hold values from 0 to 31, as said below
- route_weight: float32 [4096, 8], P(('groups', 'mix')), parts along dimension 0, may hold values from 0.1 to 0.4
- placement: int32 [32], replicated, may hold values from 0 to 31, each once
- w_gate: bfloat16 [32, 2048, 768], P('mix'), may hold values from -0.125 to 0.125
- w_up: bfloat16 [32, 2048, 768], P('mix'), may hold values from -0.125 to 0.125
- w_down: bfloat16 [32, 768, 2048], P('mix'), may hold values from -0.21875 to 0.21875
Outputs:
- layer_out: bfloat16 [4096, 2048], P(('groups', 'mix')), parts along dimension 0
There are 2 independent parts, one for each index of `groups`. A program takes and returns all parts, laid end to end along the dimension named above; an argument that names none is the same for every part. Nothing has to cross between parts.
Inputs may be any that keep to these rules, and one draw needn't show every extreme that they name: `expert_ids`: each row names 8 different experts. Within each aligned block of 128 rows (one device's rows), 8 experts appear exactly 64 times each, 8 others 64 / 2 times each and the rest 64 / 4 times each; each of the three sets is the same in every block. `placement`: each slot once. `lengths`: requests fill the 2048 positions in order.
All inputs are finite; a program needn't handle non-finite values.
Results may differ from a plain program's by a relative error of at most 0.013.
Values may be sent and summed in bfloat16 or wider, within the bound.
A program may use at most 128 MiB of HBM per device.

v0:
```python
import jax
import jax.numpy as jnp
from jax import lax
from jax.sharding import PartitionSpec as P

HEADS = 64
HEAD_DIM = 64
SPAN = 256


epsilon = 1e-05


def request_layout(lengths, tokens_total):
    request_end = jnp.cumsum(lengths)
    request_first = request_end - lengths
    position = jnp.arange(tokens_total, dtype=jnp.int32)
    segment = jnp.sum((position[None, :] >= request_end[:, None]).astype(jnp.int32), axis=0)
    member = segment[None, :] == jnp.arange(lengths.shape[0], dtype=jnp.int32)[:, None]
    first_of = jnp.sum(jnp.where(member, request_first[:, None], 0), axis=0)
    return (segment, first_of, member)


def scan_heads(
    head_values,
    head_steps,
    head_rates,
    in_basis,
    out_basis,
    state_init,
    segment,
    first_of,
    member,
    block_len,
):
    tokens_total = head_values.shape[0]
    local_heads = head_steps.shape[0]
    head_width = head_values.shape[1] // local_heads
    blocks = tokens_total // block_len
    highest = lax.Precision.HIGHEST
    log_decay = -head_steps * head_rates[:, None]
    driven = (
        head_values.reshape(tokens_total, local_heads, head_width)
        .transpose(1, 0, 2)
        .astype(jnp.float32)
    )
    driven = driven * head_steps[:, :, None]
    drive_split = driven.reshape(local_heads, blocks, block_len, head_width).transpose(1, 0, 2, 3)
    decay_split = log_decay.reshape(local_heads, blocks, block_len).transpose(1, 0, 2)

    def split_rows(array):
        return array.reshape((blocks, block_len) + array.shape[1:])

    block_first = jnp.arange(blocks, dtype=jnp.int32) * block_len
    member_blocks = member.reshape(member.shape[0], blocks, block_len).transpose(1, 0, 2)
    init_heads = state_init.transpose(1, 0, 2, 3)
    inputs = (
        drive_split,
        decay_split,
        split_rows(in_basis),
        split_rows(out_basis),
        split_rows(segment),
        split_rows(first_of),
        member_blocks,
        block_first,
    )
    offsets = jnp.arange(block_len, dtype=jnp.int32)
    causal = offsets[None, :] <= offsets[:, None]

    def advance(states_in, block_in):
        (
            drive_heads,
            decay_heads,
            basis_block,
            readout_block,
            segment_block,
            first_block,
            member_block,
            first_pos,
        ) = block_in
        basis_wide = basis_block.astype(jnp.float32)
        readout_wide = readout_block.astype(jnp.float32)
        same_seq = (segment_block[:, None] == segment_block[None, :]) & causal
        scores = jnp.dot(readout_block, basis_block.T, preferred_element_type=jnp.float32)
        carried = first_block < first_pos
        member_wide = member_block.astype(jnp.float32)

        def one_head(state_in, drive_block, decay_block, head_init):
            running = jnp.cumsum(decay_block)
            earlier = running - decay_block
            gap_values = jnp.minimum(running[:, None] - running[None, :], 0.0)
            kernel = jnp.where(same_seq, jnp.exp(gap_values), 0.0)
            output = jnp.dot(kernel * scores, drive_block, precision=highest)
            before = jnp.max(jnp.where(same_seq, earlier[None, :], -jnp.inf), axis=1)
            weight = jnp.exp(running - before)
            from_state = jnp.dot(readout_wide, state_in.T, precision=highest)
            projected = jnp.einsum("qn,rpn->rqp", readout_wide, head_init, precision=highest)
            from_init = jnp.sum(member_wide[:, :, None] * projected, axis=0)
            output = output + weight[:, None] * jnp.where(carried[:, None], from_state, from_init)
            last_weight = jnp.where(same_seq[-1], jnp.exp(running[-1] - running), 0.0)
            state_out = jnp.dot(
                (drive_block * last_weight[:, None]).T, basis_wide, precision=highest
            )
            init_last = jnp.einsum("r,rpn->pn", member_wide[:, -1], head_init, precision=highest)
            source = jnp.where(carried[-1], state_in, init_last)
            state_out = state_out + weight[-1] * source
            return (state_out, output)

        return jax.vmap(one_head)(states_in, drive_heads, decay_heads, init_heads)

    empty_state = jnp.zeros((local_heads, head_width, in_basis.shape[1]), jnp.float32)
    _, outputs = lax.scan(advance, empty_state, inputs)
    return outputs.transpose(0, 2, 1, 3).reshape(tokens_total, local_heads * head_width)


def local(
    resid_in,
    head_in,
    gate_in,
    in_basis,
    out_basis,
    step_size,
    decay_rate,
    init_state,
    lengths,
    norm_gain,
    out_proj,
    moe_gain,
    expert_ids,
    route_weight,
    placement,
    w_gate,
    w_up,
    w_down,
):
    tokens_total = head_in.shape[0]
    model_width = out_proj.shape[1]
    devices = lax.axis_size("mix")
    tok_rows = tokens_total // devices
    segment, first_of, member = request_layout(lengths, tokens_total)
    scan_out = scan_heads(
        head_in,
        step_size,
        decay_rate,
        in_basis,
        out_basis,
        init_state,
        segment,
        first_of,
        member,
        SPAN,
    )
    gated_out = scan_out * jax.nn.silu(gate_in.astype(jnp.float32))
    regrouped = lax.all_to_all(
        gated_out.astype(jnp.bfloat16), "mix", split_axis=0, concat_axis=1, tiled=True
    ).astype(gated_out.dtype)
    squares = jnp.sum(regrouped * regrouped, axis=1)
    mixed_in = (regrouped * norm_gain).astype(jnp.bfloat16)
    full_proj = lax.all_gather(out_proj, "mix", axis=0, tiled=True)
    group_terms = jnp.einsum(
        "tgc,gcd->tgd",
        mixed_in.reshape(tok_rows, devices, -1),
        full_proj.reshape(devices, -1, model_width),
        preferred_element_type=jnp.float32,
    ).astype(jnp.bfloat16)
    group_terms = lax.optimization_barrier(group_terms)
    mixer_sum = jnp.sum(group_terms.astype(jnp.float32), axis=1)
    mixer_out = mixer_sum * lax.rsqrt(squares / (HEADS * HEAD_DIM) + epsilon)[:, None]
    hidden = resid_in.astype(jnp.float32) + mixer_out
    normed = (
        hidden * lax.rsqrt(jnp.mean(hidden * hidden, axis=1, keepdims=True) + epsilon) * moe_gain
    ).astype(jnp.bfloat16)
    top_count = expert_ids.shape[1]
    flat_ids = expert_ids.reshape(-1)
    pair_count = flat_ids.shape[0]
    experts_total = placement.shape[0]
    cap_slots = 2 * pair_count // experts_total
    choose = (flat_ids[:, None] == jnp.arange(experts_total, dtype=jnp.int32)[None, :]).astype(
        jnp.int32
    )
    slot_of = jnp.sum(choose * placement[None, :], axis=1)
    slot_rank = jnp.sum(jnp.cumsum(choose, axis=0) * choose, axis=1) - 1
    buffer_index = slot_of * cap_slots + slot_rank
    owner_token = (
        jnp.full((experts_total * cap_slots,), -1, jnp.int32)
        .at[buffer_index]
        .set(jnp.arange(pair_count, dtype=jnp.int32) // top_count)
    )
    filled = owner_token >= 0
    send_rows = jnp.where(
        filled[:, None],
        jnp.take(normed, jnp.maximum(owner_token, 0), axis=0),
        jnp.zeros((), jnp.bfloat16),
    )
    send_rows = send_rows.reshape(devices, experts_total // devices, cap_slots, model_width)
    received = lax.all_to_all(send_rows, "mix", split_axis=0, concat_axis=0, tiled=True)
    gate_part = jnp.einsum("sekd,edf->sekf", received, w_gate, preferred_element_type=jnp.float32)
    up_part = jnp.einsum("sekd,edf->sekf", received, w_up, preferred_element_type=jnp.float32)
    inner_act = (jax.nn.silu(gate_part) * up_part).astype(jnp.bfloat16)
    result = jnp.einsum(
        "sekf,efd->sekd", inner_act, w_down, preferred_element_type=jnp.float32
    ).astype(jnp.bfloat16)
    returned_rows = lax.all_to_all(result, "mix", split_axis=0, concat_axis=0, tiled=True)
    back_flat = returned_rows.reshape(experts_total * cap_slots, model_width)
    picked = jnp.take(back_flat, buffer_index, axis=0).reshape(tok_rows, top_count, model_width)
    expert_sum = jnp.sum(route_weight[:, :, None] * picked.astype(jnp.float32), axis=1)
    return (hidden + expert_sum).astype(jnp.bfloat16)


def solution(mesh):
    return jax.shard_map(
        local,
        mesh=mesh,
        in_specs=(
            P(("groups", "mix"), None),
            P("groups", "mix"),
            P("groups", "mix"),
            P("groups", None),
            P("groups", None),
            P("mix", "groups"),
            P("mix"),
            P("groups", "mix", None, None),
            P("groups"),
            P(),
            P("mix", None),
            P(),
            P(("groups", "mix"), None),
            P(("groups", "mix"), None),
            P(),
            P("mix", None, None),
            P("mix", None, None),
            P("mix", None, None),
        ),
        out_specs=P(("groups", "mix"), None),
        check_vma=False,
    )
```

profile of v0, /device:TPU:15, one launch (start us, length us, event | category | flops | bytes accessed | tf_op | source)
XLA Modules:
  0.0 655.9 jit_solution(5398734231998708079)
XLA Ops:
  11.5 2.2 copy.110
  15.5 123.2 %while.13 = (s32[]{:T(128)}, f32[4,64,128]{2,1,0:T(8,128)S(1)}, f32[8,4,256,64]{2,3,1,0:T(8,128)}, f32[8,4,256,64]{2,0,3,1:T(8,128)}, s32[8,256]{1,0:T(8,128)S(1...) while((s32[]{:T(128)}, f32[4,64,128]{2,1,0:T(8,128)S(1)}, ...), condition=%wide.region_8.9_spmd.clone, body=%wide.region_3.8_spmd.clone.sunk | while | flops 1231164672 | bytes 6564249 | solution.py:112
  17.8 1.9 fusion.115
  23.2 1.8 constant_dynamic-slice_fusion.7
  25.0 2.2 fusion.116
  29.1 1.7 convolution_add_fusion.3
  33.2 1.9 fusion.115
  38.6 1.8 constant_dynamic-slice_fusion.7
  40.4 2.1 fusion.116
  48.6 1.9 fusion.115
  53.9 1.8 constant_dynamic-slice_fusion.7
  55.7 2.2 fusion.116
  64.0 1.9 fusion.115
  69.3 1.8 constant_dynamic-slice_fusion.7
  71.1 2.2 fusion.116
  75.3 1.7 convolution_add_fusion.3
  79.4 1.9 fusion.115
  84.7 1.8 constant_dynamic-slice_fusion.7
  86.5 2.2 fusion.116
  90.7 1.7 convolution_add_fusion.3
  94.8 1.9 fusion.115
  100.1 1.8 constant_dynamic-slice_fusion.7
  101.9 2.1 fusion.116
  110.1 1.9 fusion.115
  115.5 1.9 constant_dynamic-slice_fusion.7
  117.4 2.1 fusion.116
  125.6 1.9 fusion.115
  130.9 1.8 constant_dynamic-slice_fusion.7
  132.8 2.2 fusion.116
  138.6 2.9 copy.89
  143.9 1.9 fusion.62
  147.1 6.6 %all-to-all-start = ((bf16[16,128,256]{2,1,0:T(8,128)(2,1)}), bf16[16,128,256]{2,1,0:T(8,128)(2,1)S(1)}, u32[]{:S(2)}, u32[]{:S(2)}) async-start(bf16[16,128,256]{2,1,0:T(8,128)(2,1)} %bitcast.11), calls=%async_computation | async-start | bytes 2097152 | tf_op jit(solution)/shard_map/all_to_all | solution.py:154
  154.0 9.0 %reduce-window.26 = s32[32,8,128]{2,1,0:T(8,128)S(1)} reduce-window(s32[32,8,128]{2,1,0:T(8,128)S(1)} %fusion.68, s32[]{:T(128)} %constant.97.clone.1), window={size=1x1x128 pad=0_0x0_0x127_0}, to_apply=%region_12.13 | reduce-window | flops 4161536 | bytes 262148 | tf_op jit(solution)/shard_map/reduce-window.3
  163.7 4.3 scatter_custom_fusion
  168.2 10.4 %all-to-all-done = bf16[16,128,256]{2,1,0:T(8,128)(2,1)S(1)} async-done(((bf16[16,128,256]{2,1,0:T(8,128)(2,1)}), bf16[16,128,256]{2,1,0:T(8,128)(2,1)S(1)}, u32[]{:S(2)}, u32[]{:S(2)}) %all-to-all-start) | async-done | bytes 1048608 | tf_op jit(solution)/shard_map/all_to_all | solution.py:154
  178.9 11.4 %convert_bitcast_fusion.1 = bf16[128,16,2048]{2,0,1:T(8,128)(2,1)} fusion(bf16[16,256,2048]{2,1,0:T(8,128)(2,1)} %bitcast.224, bf16[16,128,256]{2,1,0:T(8,128)(2,1)S(1)} %all-to-all-done, f32[16,256]{1,0:T(8,128)S(1)} %mul.163), kind=kOutput, calls=%fused_computation.66 | convolution fusion | flops 2153250816 | bytes 26230784 | tf_op jit(solution)/shard_map/tgc,gcd->tgd/dot_general | solution.py:160
  190.3 5.3 convert_reduce_fusion
  196.3 11.0 %gather_fusion = bf16[2048,2048]{1,0:T(8,128)(2,1)} fusion(bf16[128,2048]{1,0:T(8,128)(2,1)S(1)} %multiply_convert_fusion, s32[2048]{0:T(1024)S(1)} %maximum_clamp_fusion), kind=kCustom, calls=%fused_computation | custom fusion | bytes 16785408 | tf_op jit(solution)/shard_map/jit(_take)/gather | solution.py:192
  207.3 4.6 select_select_fusion
  212.0 187.1 %all_to_all.23 = bf16[16,2,64,2048]{3,2,1,0:T(8,128)(2,1)S(1)} all-to-all(bf16[16,2,64,2048]{3,2,1,0:T(8,128)(2,1)S(1)} %select_select_fusion), channel_id=1, replica_groups=mesh['groups'=2,'mix'=16] {'mix'}, dimensions={0} | all-to-all | bytes 16777216 | tf_op jit(solution)/shard_map/all_to_all | solution.py:196
  399.1 10.6 %fusion.39 = f32[2,16,64,768]{3,2,1,0:T(8,128)} fusion(bf16[16,2,64,2048]{3,2,1,0:T(8,128)(2,1)S(1)} %all_to_all.23, bf16[2,2048,768]{2,1,0:T(8,128)(2,1)} %param.36), kind=kOutput, calls=%fused_computation.67 | convolution fusion | flops 6442450944 | bytes 20971520 | tf_op jit(solution)/shard_map/sekd,edf->sekf/dot_general | solution.py:198
  409.7 8.5 %fusion.41 = f32[2,16,64,768]{3,2,1,0:T(8,128)} fusion(bf16[16,2,64,2048]{3,2,1,0:T(8,128)(2,1)S(1)} %all_to_all.23, bf16[2,2048,768]{2,1,0:T(8,128)(2,1)S(1)} %bitcast.249), kind=kOutput, calls=%fused_computation.69 | convolution fusion | flops 6442450944 | bytes 20971520 | tf_op jit(solution)/shard_map/sekd,edf->sekf/dot_general | solution.py:197
  418.2 14.5 %convert_bitcast_fusion = bf16[16,2,64,2048]{3,2,0,1:T(8,128)(2,1)} fusion(bf16[2,768,2048]{2,1,0:T(8,128)(2,1)} %param.37, f32[2,16,64,768]{3,2,1,0:T(8,128)} %fusion.39, f32[2,16,64,768]{3,2,1,0:T(8,128)} %fusion.41), kind=kOutput, calls=%fused_computation.64 | convolution fusion | flops 6456082432 | bytes 27262976 | tf_op jit(solution)/shard_map/sekf,efd->sekd/dot_general | solution.py:200
  432.7 8.3 %copy.99 = bf16[16,2,64,2048]{3,2,1,0:T(8,128)(2,1)} copy(bf16[16,2,64,2048]{3,2,0,1:T(8,128)(2,1)} %convert_bitcast_fusion) | data formatting | bytes 16777216 | tf_op jit(solution)/shard_map/convert_element_type | solution.py:202
  441.0 5.8 all-to-all-start.2
  447.0 182.1 %all-to-all-done.2 = bf16[16,2,64,2048]{3,2,1,0:T(8,128)(2,1)} async-done(((bf16[16,2,64,2048]{3,2,1,0:T(8,128)(2,1)}), bf16[16,2,64,2048]{3,2,1,0:T(8,128)(2,1)}, u32[]{:S(2)}, u32[]{:S(2)}) %all-to-all-start.2) | async-done | bytes 8388640 | tf_op jit(solution)/shard_map/all_to_all | solution.py:203
  629.2 13.3 %gather_fusion.1 = bf16[1024,2048]{1,0:T(8,128)(2,1)} fusion(bf16[2048,2048]{1,0:T(8,128)(2,1)} %bitcast.29, s32[1024]{0:T(1024)S(1)} %broadcast_clamp_fusion), kind=kCustom, calls=%fused_computation.1 | custom fusion | bytes 8392704 | tf_op jit(solution)/shard_map/jit(_take)/gather | solution.py:205
  642.4 5.6 multiply_reduce_fusion
  (293 shorter events, 84.1 us)
Async XLA Ops:
  6.5 8.8 %copy-start.2 = (f32[4,2048]{1,0:T(4,128)S(1)}, f32[4,2048]{1,0:T(4,128)}, u32[]{:S(2)}) copy-start(f32[4,2048]{1,0:T(4,128)} %param.25) | copy-start | bytes 98308
  6.5 8.9 %copy-start.7 = (f32[4]{0:T(128)S(1)}, f32[4]{0:T(128)}, u32[]{:S(2)}) copy-start(f32[4]{0:T(128)} %param.26) | copy-start | bytes 52
  6.5 172.4 %all-gather.2.cloned.1.call-start = ((), (), s32[]{:S(2)}) async-start(), calls=%async_computation.3 | async-start | bytes 17825792 | tf_op jit(solution)/shard_map/all_gather | solution.py:159
  138.6 3.8 copy-start.1
  142.4 11.3 %copy-start.5 = (s32[128,8]{0,1:T(8,128)S(1)}, s32[128,8]{0,1:T(8,128)}, u32[]{:S(2)}) copy-start(s32[128,8]{0,1:T(8,128)} %param.32) | copy-start | bytes 12292
  142.5 11.6 %copy-start.3 = (f32[4096]{0:T(1024)S(1)}, f32[4096]{0:T(1024)}, u32[]{:S(2)}) copy-start(f32[4096]{0:T(1024)} %param.29) | copy-start | bytes 49156
  142.5 21.1 %copy-start.8 = (s32[32]{0:T(128)S(1)}, s32[32]{0:T(128)}, u32[]{:S(2)}) copy-start(s32[32]{0:T(128)} %param.34) | copy-start | bytes 388
  147.1 31.5 %all-to-all-start = ((bf16[16,128,256]{2,1,0:T(8,128)(2,1)}), bf16[16,128,256]{2,1,0:T(8,128)(2,1)S(1)}, u32[]{:S(2)}, u32[]{:S(2)}) async-start(bf16[16,128,256]{2,1,0:T(8,128)(2,1)} %bitcast.11), calls=%async_computation | async-start | bytes 2097152 | tf_op jit(solution)/shard_map/all_to_all | solution.py:154
  190.3 5.4 copy-start
  190.3 5.7 copy-start.4
  211.9 197.8 %slice-start = ((s8[6291456]{0:T(1024)(128)(4,1)}), s8[4194304]{0:T(1024)(128)(4,1)S(1)}, s32[]{:S(2)}) async-start(s8[6291456]{0:T(1024)(128)(4,1)} %bitcast.248), calls=%async_computation.4 | async-start | bytes 8388608
  399.1 10.6 %slice-start.1 = ((s8[6291456]{0:T(1024)(128)(4,1)}), s8[2097152]{0:T(1024)(128)(4,1)S(1)}, s32[]{:S(2)}) async-start(s8[6291456]{0:T(1024)(128)(4,1)} %bitcast.248), calls=%async_computation.5 | async-start | bytes 4194304
  441.0 5.9 copy-start.6
  441.0 188.2 %all-to-all-start.2 = ((bf16[16,2,64,2048]{3,2,1,0:T(8,128)(2,1)}), bf16[16,2,64,2048]{3,2,1,0:T(8,128)(2,1)}, u32[]{:S(2)}, u32[]{:S(2)}) async-start(bf16[16,2,64,2048]{3,2,1,0:T(8,128)(2,1)} %copy.99), calls=%async_computation.2 | async-start | bytes 16777216 | tf_op jit(solution)/shard_map/all_to_all | solution.py:203
Sparse Core Ops, SparseCore 0:
  9.5 125.6 all-gather.1
where the time goes:
time: 658 us; the launch traced here: 656 us
  waiting for transfers between devices  193 us (29%)
  blocking collectives  187 us (28%)
  matrix products  118 us (18%)
  local copies, waits for them, and re-layouts  79.7 us (12%)
  other arithmetic  51.1 us (8%)
  between operations  13.8 us (2%)
  starting transfers between devices  12.4 us (2%)
    all_to_all x1, blocking collectives, local(): lax.all_to_all(send_rows, 'mix', split_axis=0, concat_axis=0, tiled=True)  187 us
    all_to_all x1, waiting for transfers between devices, local(): lax.all_to_all(result, 'mix', split_axis=0, concat_axis=0, tiled=True)  182 us
    another operation x20, other arithmetic  20.1 us
    dynamic_slice x32, local copies, waits for them, and re-layouts, scan_heads(): _, outputs = lax.scan(advance, empty_state, inputs)  19.5 us
    dot_general x8, matrix products, one_head(): output = jnp.dot(kernel * scores, drive_block, precision=highest)  17.2 us
    dot_general x8, matrix products, one_head(): jnp.einsum('qn,rpn->rqp', readout_wide, head_init, precision=highest)  14.9 us
    dot_general x1, matrix products, local(): jnp.einsum('sekf,efd->sekd', inner_act, w_down, preferred_element_type=jn...  14.5 us
    dot_general x8, matrix products, one_head(): jnp.dot((drive_block * last_weight[:, None]).T, basis_wide, precision=hig...  13.8 us
  transfers between devices with their start and end apart: 3, of which 2 were waited for; matrix products, arithmetic and copies ran while one was open for 23% of the time, Pallas kernels for 0%

commit v1 on v0

v1 whole, which is shorter than its diff:
```python
import functools

import jax
import jax.numpy as jnp
from jax import lax
from jax.experimental import pallas as pl
from jax.experimental.pallas import tpu as pltpu
from jax.sharding import PartitionSpec as P

HEADS = 64
HEAD_DIM = 64
SPAN = 256
MESH = pl.DeviceIdType.MESH
NT = (((1,), (1,)), ((), ()))
TN = (((0,), (0,)), ((), ()))

epsilon = 1e-05


def scan_kernel(
    requests,
    heads,
    width,
    first_ref,
    x_ref,
    gate_ref,
    basis_ref,
    readout_ref,
    step_ref,
    decay_ref,
    init_ref,
    gain_ref,
    mixed_ref,
    square_ref,
    state_ref,
    source_ref,
):
    block = pl.program_id(0)
    rows = x_ref.shape[0]
    lanes = heads * width
    start = block * rows
    highest = lax.Precision.HIGHEST

    @pl.when(block == 0)
    def _():
        state_ref[...] = jnp.zeros_like(state_ref)

    pos_col = start + lax.broadcasted_iota(jnp.int32, (rows, 1), 0)
    pos_row = start + lax.broadcasted_iota(jnp.int32, (1, rows), 1)
    seg_col = jnp.zeros((rows, 1), jnp.int32)
    seg_row = jnp.zeros((1, rows), jnp.int32)
    seg_first = jnp.int32(0)
    seg_last = jnp.int32(0)
    for r in range(1, requests):
        first = first_ref[r]
        seg_col += (pos_col >= first).astype(jnp.int32)
        seg_row += (pos_row >= first).astype(jnp.int32)
        seg_first += (start >= first).astype(jnp.int32)
        seg_last += (start + rows - 1 >= first).astype(jnp.int32)
    carries = first_ref[seg_first] < start
    carries_last = first_ref[seg_last] < start
    same = (seg_col == seg_row) & (pos_row <= pos_col)
    total_col = lax.dot_general(
        same.astype(jnp.float32),
        decay_ref[...],
        NT,
        precision=highest,
        preferred_element_type=jnp.float32,
    )
    total_row = total_col.T
    step_row = step_ref[...]
    step_col = step_row.T
    readout = readout_ref[...]
    basis = basis_ref[...]
    scores = lax.dot_general(readout, basis, NT, preferred_element_type=jnp.float32)
    scores = jnp.where(same, scores, 0.0)

    def read(state):
        high = state.astype(jnp.bfloat16)
        low = (state - high.astype(jnp.float32)).astype(jnp.bfloat16)
        return lax.dot_general(
            readout, high, NT, preferred_element_type=jnp.float32
        ) + lax.dot_general(readout, low, NT, preferred_element_type=jnp.float32)

    carried = (seg_col == seg_first) & carries
    source_ref[...] = jnp.where(carried, read(state_ref[...]), 0.0)
    for r in range(requests):
        first = first_ref[r]

        @pl.when((first >= start) & (first < start + rows))
        def _(r=r):
            source_ref[...] += jnp.where(seg_col == r, read(init_ref[r]), 0.0)

    lane = lax.broadcasted_iota(jnp.int32, (1, lanes), 1)

    def spread(columns):
        out = columns[:, 0:1]
        for h in range(1, heads):
            out = jnp.where(lane >= h * width, columns[:, h : h + 1], out)
        return jnp.broadcast_to(out, (columns.shape[0], lanes))

    x = x_ref[...]
    parts = []
    for h in range(heads):
        gap = jnp.minimum(total_col[:, h : h + 1] - total_row[h : h + 1, :], 0.0)
        weight = jnp.exp(gap) * scores * step_row[h : h + 1, :]
        parts.append(
            jnp.dot(
                weight.astype(jnp.bfloat16),
                x[:, h * width : (h + 1) * width],
                preferred_element_type=jnp.float32,
            )
        )
    out = jnp.concatenate(parts, axis=1)
    out = out + spread(jnp.exp(total_col)) * source_ref[...]

    gate = gate_ref[...].astype(jnp.float32)
    gated = out * (gate / (1.0 + jnp.exp(-gate)))
    square_ref[...] = lax.dot_general(
        jnp.ones((8, lanes), jnp.float32),
        gated * gated,
        NT,
        precision=highest,
        preferred_element_type=jnp.float32,
    )
    mixed_ref[...] = (gated * gain_ref[...]).astype(jnp.bfloat16)

    last = total_col[rows - 1 : rows, :]
    keep = jnp.where(
        seg_col == seg_last, jnp.exp(jnp.minimum(last - total_col, 0.0)), 0.0
    )
    drive = (x.astype(jnp.float32) * spread(keep * step_col)).astype(jnp.bfloat16)
    added = lax.dot_general(drive, basis, TN, preferred_element_type=jnp.float32)
    fade = jnp.exp(last)
    for h in range(heads):
        at = slice(h * width, (h + 1) * width)
        source = jnp.where(carries_last, state_ref[at, :], init_ref[seg_last, at, :])
        state_ref[at, :] = added[at, :] + fade[:, h : h + 1] * source


def scan(head_in, gate_in, in_basis, out_basis, step_size, decay_rate, init_state, lengths, gain):
    tokens, lanes = head_in.shape
    heads = step_size.shape[0]
    width = lanes // heads
    requests = lengths.shape[0]
    states = in_basis.shape[1]
    rows = SPAN
    order = jnp.arange(requests, dtype=jnp.int32)
    first = jnp.sum(jnp.where(order[None, :] < order[:, None], lengths[None, :], 0), axis=1)
    extra = (-heads) % 8
    step = jnp.pad(step_size, ((0, extra), (0, 0)))
    decay = jnp.pad(-step_size * decay_rate[:, None], ((0, extra), (0, 0)))
    padded = heads + extra
    init = init_state.reshape(requests, lanes, states)
    return pl.pallas_call(
        functools.partial(scan_kernel, requests, heads, width),
        grid=(tokens // rows,),
        in_specs=[
            pl.BlockSpec(memory_space=pltpu.SMEM),
            pl.BlockSpec((rows, lanes), lambda b: (b, 0)),
            pl.BlockSpec((rows, lanes), lambda b: (b, 0)),
            pl.BlockSpec((rows, states), lambda b: (b, 0)),
            pl.BlockSpec((rows, states), lambda b: (b, 0)),
            pl.BlockSpec((padded, rows), lambda b: (0, b)),
            pl.BlockSpec((padded, rows), lambda b: (0, b)),
            pl.BlockSpec((requests, lanes, states), lambda b: (0, 0, 0)),
            pl.BlockSpec((1, lanes), lambda b: (0, 0)),
        ],
        out_specs=[
            pl.BlockSpec((rows, lanes), lambda b: (b, 0)),
            pl.BlockSpec((8, rows), lambda b: (0, b)),
        ],
        out_shape=[
            jax.ShapeDtypeStruct((tokens, lanes), jnp.bfloat16),
            jax.ShapeDtypeStruct((8, tokens), jnp.float32),
        ],
        scratch_shapes=[
            pltpu.VMEM((lanes, states), jnp.float32),
            pltpu.VMEM((rows, lanes), jnp.float32),
        ],
        compiler_params=pltpu.CompilerParams(vmem_limit_bytes=40 * 2**20),
        name="scan",
    )(first, head_in, gate_in, in_basis, out_basis, step, decay, init, gain)


def ring_of(ring):
    me = lax.axis_index("mix")
    core = me % 2
    pair = me // 2
    side = pair % 2
    along = pair // 2
    place = (1 - side) * along + side * (ring - 1 - along)
    return me, core, place, 1 - 2 * core


def device_at(place, core, ring):
    far = place // (ring // 2)
    along = (1 - far) * place + far * (ring - 1 - place)
    return (2 * along + far) * 2 + core


def greet(devices):
    barrier = pltpu.get_barrier_semaphore()
    for device in devices:
        pl.semaphore_signal(barrier, inc=1, device_id={"mix": device}, device_id_type=MESH)
    pl.semaphore_wait(barrier, len(devices))


def remote(src, dst, send, recv, device):
    return pltpu.make_async_remote_copy(
        src_ref=src,
        dst_ref=dst,
        send_sem=send,
        recv_sem=recv,
        device_id={"mix": device},
        device_id_type=MESH,
    )


def gather_kernel(ring, cuts, x_ref, out_ref, local_sem, ring_send, ring_recv, pair_send, pair_recv):
    me, core, place, way = ring_of(ring)
    rows = x_ref.shape[0]
    piece = rows // cuts
    onward = device_at((place + way + ring) % ring, core, ring)
    behind = device_at((place - way + ring) % ring, core, ring)
    twin = 2 * (me // 2) + 1 - core
    greet([onward, behind, twin])
    own = pltpu.make_async_copy(x_ref, out_ref.at[pl.ds(me * rows, rows), :], local_sem)
    own.start()
    ring_copies = {}
    pair_copies = {}
    for step in range(ring):
        holder = device_at((place - step * way + 2 * ring) % ring, core, ring)
        for c in range(cuts):
            at = out_ref.at[pl.ds(holder * rows + c * piece, piece), :]
            if step > 0:
                ring_copies[step - 1, c].wait_recv()
            src = x_ref.at[pl.ds(c * piece, piece), :] if step == 0 else at
            if step < ring - 1:
                copy = remote(src, at, ring_send.at[step, c], ring_recv.at[step, c], onward)
                copy.start()
                ring_copies[step, c] = copy
            copy = remote(src, at, pair_send.at[step, c], pair_recv.at[step, c], twin)
            copy.start()
            pair_copies[step, c] = copy
    own.wait()
    for copy in ring_copies.values():
        copy.wait_send()
    for copy in pair_copies.values():
        copy.wait_send()
        copy.wait_recv()


def gather_rows(x, devices, collective_id):
    rows, columns = x.shape
    ring = devices // 2
    cuts = 2
    return pl.pallas_call(
        functools.partial(gather_kernel, ring, cuts),
        in_specs=[pl.BlockSpec(memory_space=pltpu.VMEM)],
        out_specs=pl.BlockSpec(memory_space=pl.ANY),
        out_shape=jax.ShapeDtypeStruct((devices * rows, columns), x.dtype),
        scratch_shapes=[
            pltpu.SemaphoreType.DMA,
            pltpu.SemaphoreType.DMA((ring, cuts)),
            pltpu.SemaphoreType.DMA((ring, cuts)),
            pltpu.SemaphoreType.DMA((ring, cuts)),
            pltpu.SemaphoreType.DMA((ring, cuts)),
        ],
        compiler_params=pltpu.CompilerParams(
            collective_id=collective_id, has_side_effects=True, vmem_limit_bytes=48 * 2**20
        ),
        name="gather_rows",
    )(x)


def reduce_kernel(
    ring,
    cuts,
    product,
    *refs,
):
    if product:
        mixed_ref, proj_ref, out_ref = refs[:3]
        refs = refs[3:]
        to_twin, mine, from_twin, sent, got = refs[:5]
        refs = refs[5:]
    else:
        terms_ref, out_ref = refs[:2]
        refs = refs[2:]
        mine, from_twin, sent, got = refs[:4]
        mine_sem = refs[-1]
        refs = refs[4:]
    pair_send, pair_recv, ring_send, ring_recv = refs[:4]
    me, core, place, way = ring_of(ring)
    rows = out_ref.shape[0]
    piece = rows // cuts
    onward = device_at((place + way + ring) % ring, core, ring)
    behind = device_at((place - way + ring) % ring, core, ring)
    twin = 2 * (me // 2) + 1 - core
    greet([onward, behind, twin])
    pair_copies = []
    mine_copies = []

    def give(step):
        theirs = device_at((place + (1 + step) * way) % ring, 1 - core, ring)
        if product:
            to_twin[step] = jnp.dot(
                mixed_ref[pl.ds(theirs * rows, rows), :],
                proj_ref[...],
                preferred_element_type=jnp.float32,
            ).astype(jnp.bfloat16)
            src = to_twin.at[step]
        else:
            src = terms_ref.at[pl.ds(theirs * rows, rows), :]
        copy = remote(src, from_twin.at[step], pair_send.at[step], pair_recv.at[step], twin)
        copy.start()
        pair_copies.append(copy)
        ours = device_at((place - (1 + step) * way + 2 * ring) % ring, core, ring)
        if product:
            mine[step] = jnp.dot(
                mixed_ref[pl.ds(ours * rows, rows), :],
                proj_ref[...],
                preferred_element_type=jnp.float32,
            ).astype(jnp.bfloat16)
        else:
            copy = pltpu.make_async_copy(
                terms_ref.at[pl.ds(ours * rows, rows), :], mine.at[step], mine_sem.at[step]
            )
            copy.start()
            mine_copies.append(copy)

    if product:
        give(0)
    else:
        for step in range(ring):
            give(step)
    ring_copies = {}
    for step in range(ring):
        if product and step + 1 < ring:
            give(step + 1)
        if not product:
            mine_copies[step].wait()
        pair_copies[step].wait_recv()
        for c in range(cuts):
            at = pl.ds(c * piece, piece)
            total = mine[step, at, :].astype(jnp.float32) + from_twin[step, at, :].astype(
                jnp.float32
            )
            if step > 0:
                ring_copies[step - 1, c].wait_recv()
                total = total + got[step - 1, at, :].astype(jnp.float32)
            if step < ring - 1:
                sent[step, at, :] = total.astype(jnp.bfloat16)
                copy = remote(
                    sent.at[step, at, :],
                    got.at[step, at, :],
                    ring_send.at[step, c],
                    ring_recv.at[step, c],
                    onward,
                )
                copy.start()
                ring_copies[step, c] = copy
            else:
                out_ref[at, :] = total
    for copy in pair_copies:
        copy.wait_send()
    for copy in ring_copies.values():
        copy.wait_send()


def reduce_rows(operands, rows, columns, devices, collective_id):
    product = len(operands) == 2
    ring = devices // 2
    cuts = 2
    block = pltpu.VMEM((ring, rows, columns), jnp.bfloat16)
    short = pltpu.VMEM((ring - 1, rows, columns), jnp.bfloat16)
    return pl.pallas_call(
        functools.partial(reduce_kernel, ring, cuts, product),
        in_specs=[pl.BlockSpec(memory_space=pltpu.VMEM if product else pl.ANY)] * len(operands),
        out_specs=pl.BlockSpec(memory_space=pltpu.VMEM),
        out_shape=jax.ShapeDtypeStruct((rows, columns), jnp.float32),
        scratch_shapes=([block] if product else [])
        + [block, block, short, short]
        + [
            pltpu.SemaphoreType.DMA((ring,)),
            pltpu.SemaphoreType.DMA((ring,)),
            pltpu.SemaphoreType.DMA((ring, cuts)),
            pltpu.SemaphoreType.DMA((ring, cuts)),
        ]
        + ([] if product else [pltpu.SemaphoreType.DMA((ring,))]),
        compiler_params=pltpu.CompilerParams(
            collective_id=collective_id, has_side_effects=True, vmem_limit_bytes=52 * 2**20
        ),
        name="reduce_products" if product else "reduce_rows",
    )(*operands)


def expert_kernel(
    experts, blocks, cap, x_ref, rank_ref, rank_row_ref, weight_ref, gate_hbm, up_hbm, down_hbm,
    out_ref, gate_ref, up_ref, down_ref, sems,
):
    first = pl.program_id(0) == 0
    rows = x_ref.shape[0] // blocks

    def copies(e):
        return [
            pltpu.make_async_copy(gate_hbm.at[e], gate_ref.at[e], sems.at[e, 0]),
            pltpu.make_async_copy(up_hbm.at[e], up_ref.at[e], sems.at[e, 1]),
            pltpu.make_async_copy(down_hbm.at[e], down_ref.at[e], sems.at[e, 2]),
        ]

    @pl.when(first)
    def _():
        for e in range(experts):
            for copy in copies(e):
                copy.start()

    slot_col = lax.broadcasted_iota(jnp.int32, (cap, 1), 0)
    slot_row = lax.broadcasted_iota(jnp.int32, (1, cap), 1)
    total = [None] * blocks
    for e in range(experts):
        chosen = []
        for b in range(blocks):
            at = slice(b * rows, (b + 1) * rows)
            pick = (rank_row_ref[e : e + 1, at] == slot_col).astype(jnp.bfloat16)
            chosen.append(
                jnp.dot(pick, x_ref[at, :], preferred_element_type=jnp.float32).astype(
                    jnp.bfloat16
                )
            )
        chosen = jnp.concatenate(chosen, axis=0)

        @pl.when(first)
        def _(e=e):
            for copy in copies(e):
                copy.wait()

        gate = jnp.dot(chosen, gate_ref[e], preferred_element_type=jnp.float32)
        up = jnp.dot(chosen, up_ref[e], preferred_element_type=jnp.float32)
        act = (gate / (1.0 + jnp.exp(-gate)) * up).astype(jnp.bfloat16)
        result = jnp.dot(act, down_ref[e], preferred_element_type=jnp.float32).astype(jnp.bfloat16)
        for b in range(blocks):
            at = slice(b * rows, (b + 1) * rows)
            place = (rank_ref[at, e : e + 1] == slot_row).astype(jnp.bfloat16)
            back = jnp.dot(
                place, result[b * cap : (b + 1) * cap, :], preferred_element_type=jnp.float32
            )
            back = back * weight_ref[at, e : e + 1]
            total[b] = back if e == 0 else total[b] + back
    for b in range(blocks):
        out_ref[b * rows : (b + 1) * rows, :] = total[b].astype(jnp.bfloat16)


def run_experts(x, rank, weight, w_gate, w_up, w_down, rows, cap):
    tokens, columns = x.shape
    experts, _, hidden = w_gate.shape
    blocks = 4
    span = blocks * rows
    extra = (-experts) % 8
    rank_row = jnp.pad(rank.T, ((0, extra), (0, 0)), constant_values=-1)
    any_spec = pl.BlockSpec(memory_space=pl.ANY)
    return pl.pallas_call(
        functools.partial(expert_kernel, experts, blocks, cap),
        grid=(tokens // span,),
        in_specs=[
            pl.BlockSpec((span, columns), lambda b: (b, 0)),
            pl.BlockSpec((span, experts), lambda b: (b, 0)),
            pl.BlockSpec((experts + extra, span), lambda b: (0, b)),
            pl.BlockSpec((span, experts), lambda b: (b, 0)),
            any_spec,
            any_spec,
            any_spec,
        ],
        out_specs=pl.BlockSpec((span, columns), lambda b: (b, 0)),
        out_shape=jax.ShapeDtypeStruct((tokens, columns), jnp.bfloat16),
        scratch_shapes=[
            pltpu.VMEM(w_gate.shape, jnp.bfloat16),
            pltpu.VMEM(w_up.shape, jnp.bfloat16),
            pltpu.VMEM(w_down.shape, jnp.bfloat16),
            pltpu.SemaphoreType.DMA((experts, 3)),
        ],
        compiler_params=pltpu.CompilerParams(vmem_limit_bytes=56 * 2**20),
        name="experts",
    )(x, rank, rank_row, weight, w_gate, w_up, w_down)


def local(
    resid_in,
    head_in,
    gate_in,
    in_basis,
    out_basis,
    step_size,
    decay_rate,
    init_state,
    lengths,
    norm_gain,
    out_proj,
    moe_gain,
    expert_ids,
    route_weight,
    placement,
    w_gate,
    w_up,
    w_down,
):
    tokens_total, lanes = head_in.shape
    model_width = out_proj.shape[1]
    devices = lax.axis_size("mix")
    me = lax.axis_index("mix")
    tok_rows = tokens_total // devices
    top_count = expert_ids.shape[1]
    experts_total = placement.shape[0]
    held = w_gate.shape[0]
    cap = 2 * tok_rows * top_count // experts_total

    slots = jnp.sum(
        jnp.where(
            expert_ids[:, :, None] == jnp.arange(experts_total, dtype=jnp.int32),
            placement,
            0,
        ),
        axis=2,
    )
    all_slots = lax.all_gather(slots, "mix", axis=0, tiled=True)
    all_weights = lax.all_gather(route_weight, "mix", axis=0, tiled=True)
    hits = all_slots[:, :, None] == me * held + jnp.arange(held, dtype=jnp.int32)
    named = jnp.any(hits, axis=1)
    weight = jnp.sum(jnp.where(hits, all_weights[:, :, None], 0.0), axis=1)
    below = jnp.tril(jnp.ones((tok_rows, tok_rows), jnp.bfloat16))
    count = jnp.einsum(
        "qt,bte->bqe",
        below,
        named.reshape(devices, tok_rows, held).astype(jnp.bfloat16),
        preferred_element_type=jnp.float32,
    )
    rank = jnp.where(named, count.reshape(tokens_total, held).astype(jnp.int32) - 1, -1)

    gain = lax.dynamic_slice(norm_gain, (me * lanes,), (lanes,)).reshape(1, lanes)
    mixed, squares = scan(
        head_in, gate_in, in_basis, out_basis, step_size, decay_rate, init_state, lengths, gain
    )
    squares = lax.psum_scatter(squares[0], "mix", scatter_dimension=0, tiled=True)
    mixer_sum = reduce_rows((mixed, out_proj), tok_rows, model_width, devices, 1)
    mixer_out = mixer_sum * lax.rsqrt(squares / (HEADS * HEAD_DIM) + epsilon)[:, None]
    hidden = resid_in.astype(jnp.float32) + mixer_out
    normed = (
        hidden * lax.rsqrt(jnp.mean(hidden * hidden, axis=1, keepdims=True) + epsilon) * moe_gain
    ).astype(jnp.bfloat16)
    everyone = gather_rows(normed, devices, 2)
    terms = run_experts(everyone, rank, weight, w_gate, w_up, w_down, tok_rows, cap)
    expert_sum = reduce_rows((terms,), tok_rows, model_width, devices, 3)
    return (hidden + expert_sum).astype(jnp.bfloat16)


def solution(mesh):
    return jax.shard_map(
        local,
        mesh=mesh,
        in_specs=(
            P(("groups", "mix"), None),
            P("groups", "mix"),
            P("groups", "mix"),
            P("groups", None),
            P("groups", None),
            P("mix", "groups"),
            P("mix"),
            P("groups", "mix", None, None),
            P("groups"),
            P(),
            P("mix", None),
            P(),
            P(("groups", "mix"), None),
            P(("groups", "mix"), None),
            P(),
            P("mix", None, None),
            P("mix", None, None),
            P("mix", None, None),
        ),
        out_specs=P(("groups", "mix"), None),
        check_vma=False,
    )
```

time: 658 us -> 281 us (0.43)
  Pallas kernels: 0 us -> 199 us
  waiting for transfers between devices: 193 us -> 0 us
  blocking collectives: 187 us -> 59.9 us
  matrix products: 118 us -> 0.13 us
  local copies, waits for them, and re-layouts: 79.7 us -> 13 us
  other arithmetic: 51.1 us -> 4.45 us
  between operations: 13.8 us -> 0.76 us
  starting transfers between devices: 12.4 us -> 0 us
    pallas_call x0 -> x5, Pallas kernels: none -> 199 us  [the longest x2 92.7 us: reduce_rows(): pl.pallas_call(functools.partial(reduce_kernel, ring, cuts, product), in_...]
    all_to_all x2 -> x0, waiting for transfers between devices: 193 us -> none  [the longest x1 182 us: local(): lax.all_to_all(result, 'mix', split_axis=0, concat_axis=0, tiled=True)]
    all_to_all x1 -> x0, blocking collectives: 187 us -> none  [local(): lax.all_to_all(send_rows, 'mix', split_axis=0, concat_axis=0, tiled=True)]
    dot_general x44 -> x1, matrix products: 109 us -> 0.13 us  [local(): jnp.einsum('qt,bte->bqe', below, named.reshape(devices, tok_rows, held).a...]
    all_gather x0 -> x2, blocking collectives: none -> 37.5 us  [the longest x1 21.7 us: local(): all_weights = lax.all_gather(route_weight, 'mix', axis=0, tiled=True)]
    gather x2 -> x0, local copies, waits for them, and re-layouts: 24.3 us -> none  [the longest x1 13.3 us: local(): jnp.take(back_flat, buffer_index, axis=0)]
    unnamed x0 -> x1, blocking collectives: none -> 22.4 us
    another operation x20 -> x0, other arithmetic: 20.1 us -> none
  transfers between devices with their start and end apart: 3 -> 0, of which waited for: 2 -> 0; matrix products, arithmetic and copies ran while one was open for 23% -> 0% of each run, Pallas kernels for 0% -> 0%
where the time goes in v1:
time: 281 us; the launch traced here: 278 us
  Pallas kernels  199 us (71%)
  blocking collectives  59.9 us (21%)
  local copies, waits for them, and re-layouts  13 us (5%)
  other arithmetic  4.45 us (2%)
    pallas_call x2, Pallas kernels, reduce_rows(): pl.pallas_call(functools.partial(reduce_kernel, ring, cuts, product), in_...  92.7 us
    pallas_call x1, Pallas kernels, gather_rows(): pl.pallas_call(functools.partial(gather_kernel, ring, cuts), in_specs=[pl...  55.4 us
    pallas_call x1, Pallas kernels, run_experts(): pl.pallas_call(functools.partial(expert_kernel, experts, blocks, cap), gr...  34.8 us
    unnamed x1, blocking collectives  22.4 us
    all_gather x1, blocking collectives, local(): all_weights = lax.all_gather(route_weight, 'mix', axis=0, tiled=True)  21.7 us
    pallas_call x1, Pallas kernels, scan(): pl.pallas_call(functools.partial(scan_kernel, requests, heads, width), gr...  16.4 us
    all_gather x1, blocking collectives, local(): all_slots = lax.all_gather(slots, 'mix', axis=0, tiled=True)  15.8 us
    unnamed x17, local copies, waits for them, and re-layouts  8.05 us

profile of v1, /device:TPU:15, one launch (start us, length us, event | category | flops | bytes accessed | tf_op | source)
XLA Modules:
  0.0 277.6 jit_solution(5640502473609783370)
XLA Ops:
  0.0 0.0 copy-start.6
  0.0 0.0 copy-start.7
  0.0 1.3 dynamic-slice
  2.0 0.8 select_reduce_fusion.1.first_ref
  2.7 0.8 dynamic_slice.3
  3.5 0.8 select_reduce_fusion
  4.3 0.8 negate_multiply_fusion
  5.1 15.8 %all_gather.6 = s32[2048,8]{0,1:T(8,128)S(1)} all-gather(s32[128,8]{0,1:T(8,128)S(1)} %select_reduce_fusion), channel_id=1, replica_groups=mesh['groups'=2,'mix'=16] {'mix'}, dimensions={0}, use_global_device_ids=true | all-gather | bytes 69632 | tf_op jit(solution)/shard_map/all_gather | solution.py:526
  20.9 0.1 compare_reduce_fusion
  21.1 0.1 fusion.1
  21.2 0.6 pad.13.rank_row_ref
  21.9 21.7 %all_gather.7 = f32[2048,8]{0,1:T(8,128)S(1)} all-gather(f32[128,8]{0,1:T(8,128)} %param.31), channel_id=1, replica_groups=mesh['groups'=2,'mix'=16] {'mix'}, dimensions={0}, use_global_device_ids=true | all-gather | bytes 69632 | tf_op jit(solution)/shard_map/all_gather | solution.py:527
  43.6 0.1 fusion.2
  43.7 0.8 pad.11.step_ref
  44.4 0.0 copy-start
  44.4 1.2 copy-done
  45.7 0.0 copy-start.1
  45.7 1.2 copy-done.1
  46.9 0.0 copy-start.2
  46.9 1.2 copy-done.2
  48.1 0.0 copy-start.4
  48.1 1.0 copy-done.4
  49.2 0.0 copy-start.5
  49.2 1.0 copy-done.5
  50.2 16.4 %scan.1 = (bf16[2048,256]{1,0:T(8,128)(2,1)S(1)}, f32[8,2048]{1,0:T(8,128)S(1)}) custom-call(s32[8]{0:T(128)S(1)} %select_reduce_fusion.1.first_ref, bf16[2048,256]{1,0:T(8,128)(2,1)S(1)} %copy-done, bf16[2048,256]{1,0:T(8,128)(2,1)S(1)} %copy-done.1, bf16[2048,128]{1,0:T(8,128)(2,1)S(1)} %copy-done.4, bf16[2048,128]{1,0:T(8,128)(2,1)S(1)} %copy-done.5, ...), custom_call_target="tpu_custom_call" | custom-call | tf_op jit(solution)/shard_map/scan/pallas_call | solution.py:155
  66.7 0.0 copy-start.3
  66.7 1.0 copy-done.3
  67.6 48.0 %reduce_products.1 = f32[128,2048]{1,0:T(8,128)S(1)} custom-call(bf16[2048,256]{1,0:T(8,128)(2,1)} %copy-done.3, bf16[256,2048]{1,0:T(8,128)(2,1)} %refs_1_.1), custom_call_target="tpu_custom_call" | custom-call | tf_op jit(solution)/shard_map/reduce_products/pallas_call | solution.py:378
  115.6 22.4 %all-reduce.3 = f32[2048]{0:T(1024)S(1)} all-reduce(f32[2048]{0:T(1024)S(1)} %bitcast.25), channel_id=2, replica_groups=mesh['groups'=2,'mix'=16] {'mix'}, use_global_device_ids=true, to_apply=%region_1.2.clone | all-reduce | flops 2048 | bytes 16384
  138.1 0.1 fusion.11
  138.1 0.0 copy-done.6
  138.2 0.3 multiply_reduce_fusion
  138.5 0.0 copy-done.7
  138.5 0.3 multiply_convert_fusion.x_ref
  138.8 1.4 copy.26.weight_ref
  140.3 1.4 copy.25.rank_ref
  141.6 55.4 %gather_rows.1.x_ref = bf16[2048,2048]{1,0:T(8,128)(2,1)} custom-call(bf16[128,2048]{1,0:T(8,128)(2,1)S(1)} %multiply_convert_fusion.x_ref), custom_call_target="tpu_custom_call" | custom-call | tf_op jit(solution)/shard_map/gather_rows/pallas_call | solution.py:258
  197.0 34.8 %experts.1.refs_0_ = bf16[2048,2048]{1,0:T(8,128)(2,1)} custom-call(bf16[2048,2048]{1,0:T(8,128)(2,1)} %gather_rows.1.x_ref, s32[2048,2]{1,0:T(8,128)} %copy.25.rank_ref, s32[8,2048]{1,0:T(8,128)} %pad.13.rank_row_ref, f32[2048,2]{1,0:T(8,128)} %copy.26.weight_ref, bf16[2,2048,768]{2,1,0:T(8,128)(2,1)} %gate_hbm.1, bf16[2,2048,768]{2,1,0:T(8,128)(2,1)} %up_hbm.1, ...), custom_call_target="tpu_custom_call" | custom-call | tf_op jit(solution)/shard_map/experts/pallas_call | solution.py:463
  231.8 44.8 %reduce_rows.1 = f32[128,2048]{1,0:T(8,128)S(1)} custom-call(bf16[2048,2048]{1,0:T(8,128)(2,1)} %experts.1.refs_0_), custom_call_target="tpu_custom_call" | custom-call | tf_op jit(solution)/shard_map/reduce_rows/pallas_call | solution.py:378
  276.6 1.0 add_convert_fusion
  (5 shorter events, 0.1 us)
Async XLA Ops:
  0.0 138.1 %copy-start.6 = (bf16[128,2048]{1,0:T(8,128)(2,1)S(1)}, bf16[128,2048]{1,0:T(8,128)(2,1)}, u32[]{:S(2)}) copy-start(bf16[128,2048]{1,0:T(8,128)(2,1)} %param.18) | copy-start | bytes 1572868
  0.0 138.5 %copy-start.7 = (f32[2048]{0:T(1024)S(1)}, f32[2048]{0:T(1024)}, u32[]{:S(2)}) copy-start(f32[2048]{0:T(1024)} %param.29) | copy-start | bytes 24580
  44.4 1.2 copy-start
  45.7 1.2 copy-start.1
  46.9 1.2 copy-start.2
  48.1 1.0 copy-start.4
  49.2 1.0 copy-start.5
  66.7 1.0 copy-start.3

commit v2 on v1

--- a/solution.py
+++ b/solution.py
@@ -281,8 +281,10 @@
     *refs,
 ):
     if product:
-        mixed_ref, proj_ref, out_ref = refs[:3]
-        refs = refs[3:]
+        mixed_ref, proj_ref, side_ref, out_ref, sides_ref = refs[:5]
+        refs = refs[5:]
+        side_rows = side_ref.shape[0]
+        local_sem, side_send, side_recv, side_pair_send, side_pair_recv = refs[-5:]
         to_twin, mine, from_twin, sent, got = refs[:5]
         refs = refs[5:]
     else:
@@ -301,6 +303,28 @@
     greet([onward, behind, twin])
     pair_copies = []
     mine_copies = []
+    side_copies = {}
+    side_pairs = []
+
+    def pass_side(step):
+        holder = device_at((place - step * way + 2 * ring) % ring, core, ring)
+        at = sides_ref.at[pl.ds(holder * side_rows, side_rows), :]
+        if step > 0:
+            side_copies[step - 1].wait_recv()
+        src = side_ref if step == 0 else at
+        if step < ring - 1:
+            copy = remote(src, at, side_send.at[step], side_recv.at[step], onward)
+            copy.start()
+            side_copies[step] = copy
+        copy = remote(src, at, side_pair_send.at[step], side_pair_recv.at[step], twin)
+        copy.start()
+        side_pairs.append(copy)
+
+    if product:
+        own = pltpu.make_async_copy(
+            side_ref, sides_ref.at[pl.ds(me * side_rows, side_rows), :], local_sem
+        )
+        own.start()
 
     def give(step):
         theirs = device_at((place + (1 + step) * way) % ring, 1 - core, ring)
@@ -332,6 +356,7 @@
 
     if product:
         give(0)
+        pass_side(0)
     else:
         for step in range(ring):
             give(step)
@@ -339,6 +364,7 @@
     for step in range(ring):
         if product and step + 1 < ring:
             give(step + 1)
+            pass_side(step + 1)
         if not product:
             mine_copies[step].wait()
         pair_copies[step].wait_recv()
@@ -367,10 +393,17 @@
         copy.wait_send()
     for copy in ring_copies.values():
         copy.wait_send()
+    if product:
+        own.wait()
+        for copy in side_copies.values():
+            copy.wait_send()
+        for copy in side_pairs:
+            copy.wait_send()
+            copy.wait_recv()
 
 
 def reduce_rows(operands, rows, columns, devices, collective_id):
-    product = len(operands) == 2
+    product = len(operands) == 3
     ring = devices // 2
     cuts = 2
     block = pltpu.VMEM((ring, rows, columns), jnp.bfloat16)
@@ -378,8 +411,13 @@
     return pl.pallas_call(
         functools.partial(reduce_kernel, ring, cuts, product),
         in_specs=[pl.BlockSpec(memory_space=pltpu.VMEM if product else pl.ANY)] * len(operands),
-        out_specs=pl.BlockSpec(memory_space=pltpu.VMEM),
-        out_shape=jax.ShapeDtypeStruct((rows, columns), jnp.float32),
+        out_specs=[pl.BlockSpec(memory_space=pltpu.VMEM)] * (2 if product else 1),
+        out_shape=[jax.ShapeDtypeStruct((rows, columns), jnp.float32)]
+        + (
+            [jax.ShapeDtypeStruct((devices * operands[2].shape[0], rows), jnp.float32)]
+            if product
+            else []
+        ),
         scratch_shapes=([block] if product else [])
         + [block, block, short, short]
         + [
@@ -388,7 +426,11 @@
             pltpu.SemaphoreType.DMA((ring, cuts)),
             pltpu.SemaphoreType.DMA((ring, cuts)),
         ]
-        + ([] if product else [pltpu.SemaphoreType.DMA((ring,))]),
+        + (
+            [pltpu.SemaphoreType.DMA] + [pltpu.SemaphoreType.DMA((ring,))] * 4
+            if product
+            else [pltpu.SemaphoreType.DMA((ring,))]
+        ),
         compiler_params=pltpu.CompilerParams(
             collective_id=collective_id, has_side_effects=True, vmem_limit_bytes=52 * 2**20
         ),
@@ -523,26 +565,28 @@
         ),
         axis=2,
     )
-    all_slots = lax.all_gather(slots, "mix", axis=0, tiled=True)
-    all_weights = lax.all_gather(route_weight, "mix", axis=0, tiled=True)
-    hits = all_slots[:, :, None] == me * held + jnp.arange(held, dtype=jnp.int32)
-    named = jnp.any(hits, axis=1)
-    weight = jnp.sum(jnp.where(hits, all_weights[:, :, None], 0.0), axis=1)
-    below = jnp.tril(jnp.ones((tok_rows, tok_rows), jnp.bfloat16))
-    count = jnp.einsum(
-        "qt,bte->bqe",
-        below,
-        named.reshape(devices, tok_rows, held).astype(jnp.bfloat16),
-        preferred_element_type=jnp.float32,
-    )
-    rank = jnp.where(named, count.reshape(tokens_total, held).astype(jnp.int32) - 1, -1)
-
     gain = lax.dynamic_slice(norm_gain, (me * lanes,), (lanes,)).reshape(1, lanes)
     mixed, squares = scan(
         head_in, gate_in, in_basis, out_basis, step_size, decay_rate, init_state, lengths, gain
     )
-    squares = lax.psum_scatter(squares[0], "mix", scatter_dimension=0, tiled=True)
-    mixer_sum = reduce_rows((mixed, out_proj), tok_rows, model_width, devices, 1)
+    side = jnp.concatenate(
+        [slots.T.astype(jnp.float32), route_weight.T, squares[0].reshape(devices, tok_rows)], axis=0
+    )
+    mixer_sum, sides = reduce_rows((mixed, out_proj, side), tok_rows, model_width, devices, 1)
+    sides = sides.reshape(devices, 2 * top_count + devices, tok_rows)
+    squares = jnp.sum(
+        lax.dynamic_index_in_dim(sides, 2 * top_count + me, axis=1, keepdims=False), axis=0
+    )
+    all_slots = sides[:, :top_count, :, None].astype(jnp.int32)
+    hits = all_slots == me * held + jnp.arange(held, dtype=jnp.int32)
+    named = jnp.any(hits, axis=1)
+    weight = jnp.sum(jnp.where(hits, sides[:, top_count : 2 * top_count, :, None], 0.0), axis=1)
+    weight = weight.reshape(tokens_total, held)
+    below = jnp.tril(jnp.ones((tok_rows, tok_rows), jnp.bfloat16))
+    count = jnp.einsum(
+        "qt,bte->bqe", below, named.astype(jnp.bfloat16), preferred_element_type=jnp.float32
+    )
+    rank = jnp.where(named, count.astype(jnp.int32) - 1, -1).reshape(tokens_total, held)
     mixer_out = mixer_sum * lax.rsqrt(squares / (HEADS * HEAD_DIM) + epsilon)[:, None]
     hidden = resid_in.astype(jnp.float32) + mixer_out
     normed = (
@@ -550,7 +594,7 @@
     ).astype(jnp.bfloat16)
     everyone = gather_rows(normed, devices, 2)
     terms = run_experts(everyone, rank, weight, w_gate, w_up, w_down, tok_rows, cap)
-    expert_sum = reduce_rows((terms,), tok_rows, model_width, devices, 3)
+    (expert_sum,) = reduce_rows((terms,), tok_rows, model_width, devices, 3)
     return (hidden + expert_sum).astype(jnp.bfloat16)
 
 

time: 281 us -> 213 us (0.76)
  blocking collectives: 59.9 us -> 0 us
  Pallas kernels: 199 us -> 193 us
    all_gather x2 -> x0, blocking collectives: 37.5 us -> none  [the longest x1 21.7 us: local(): all_weights = lax.all_gather(route_weight, 'mix', axis=0, tiled=True)]
    unnamed x1 -> x0, blocking collectives: 22.4 us -> none
    pallas_call x1, Pallas kernels: 55.4 us -> 48.4 us  [gather_rows(): pl.pallas_call(functools.partial(gather_kernel, ring, cuts), in_specs=[pl...]
where the time goes in v2:
time: 213 us; the launch traced here: 210 us
  Pallas kernels  193 us (91%)
  local copies, waits for them, and re-layouts  11.7 us (5%)
  other arithmetic  5.08 us (2%)
    pallas_call x2, Pallas kernels, reduce_rows(): pl.pallas_call(functools.partial(reduce_kernel, ring, cuts, product), in_...  92.8 us
    pallas_call x1, Pallas kernels, gather_rows(): pl.pallas_call(functools.partial(gather_kernel, ring, cuts), in_specs=[pl...  48.4 us
    pallas_call x1, Pallas kernels, run_experts(): pl.pallas_call(functools.partial(expert_kernel, experts, blocks, cap), gr...  35 us
    pallas_call x1, Pallas kernels, scan(): pl.pallas_call(functools.partial(scan_kernel, requests, heads, width), gr...  16.4 us
    unnamed x17, local copies, waits for them, and re-layouts  6.78 us

profile of v2, /device:TPU:15, one launch (start us, length us, event | category | flops | bytes accessed | tf_op | source)
XLA Modules:
  0.0 209.7 jit_solution(10353411098108401606)
XLA Ops:
  0.0 0.0 copy-start.7
  0.0 0.8 select_reduce_fusion.1.first_ref
  0.8 0.8 dynamic_slice.7
  1.5 0.8 select_reduce_fusion
  2.4 0.8 negate_multiply_fusion
  3.2 0.8 pad.11.step_ref
  4.0 0.0 copy-start
  4.0 1.2 copy-done
  5.2 0.0 copy-start.1
  5.2 1.2 copy-done.1
  6.4 0.0 copy-start.2
  6.4 1.2 copy-done.2
  7.6 0.0 copy-start.4
  7.6 1.0 copy-done.4
  8.7 0.0 copy-start.5
  8.7 1.0 copy-done.5
  9.7 0.0 copy-start.6
  9.7 16.4 %scan.1 = (bf16[2048,256]{1,0:T(8,128)(2,1)S(1)}, f32[8,2048]{1,0:T(8,128)S(1)}) custom-call(s32[8]{0:T(128)S(1)} %select_reduce_fusion.1.first_ref, bf16[2048,256]{1,0:T(8,128)(2,1)S(1)} %copy-done, bf16[2048,256]{1,0:T(8,128)(2,1)S(1)} %copy-done.1, bf16[2048,128]{1,0:T(8,128)(2,1)S(1)} %copy-done.4, bf16[2048,128]{1,0:T(8,128)(2,1)S(1)} %copy-done.5, ...), custom_call_target="tpu_custom_call" | custom-call | tf_op jit(solution)/shard_map/scan/pallas_call | solution.py:155
  26.2 0.0 copy-start.3
  26.2 1.0 copy-done.3
  27.2 0.7 pad_maximum_fusion.refs_2_
  27.9 48.0 %reduce_products.1 = (f32[128,2048]{1,0:T(8,128)S(1)}, f32[512,128]{1,0:T(8,128)S(1)}) custom-call(bf16[2048,256]{1,0:T(8,128)(2,1)} %copy-done.3, bf16[256,2048]{1,0:T(8,128)(2,1)} %refs_1_.1, f32[32,128]{1,0:T(8,128)S(1)} %pad_maximum_fusion.refs_2_), custom_call_target="tpu_custom_call" | custom-call | tf_op jit(solution)/shard_map/reduce_products/pallas_call | solution.py:411
  76.0 0.1 fusion.4
  76.1 0.1 compare_reduce_fusion
  76.2 0.0 copy-done.6
  76.2 0.3 multiply_reduce_fusion
  76.6 0.1 fusion.3
  76.8 0.6 pad.13.rank_row_ref
  77.4 0.0 copy-done.7
  77.4 0.3 multiply_convert_fusion.x_ref
  77.7 1.4 copy.23
  79.2 1.4 copy.24.rank_ref
  80.5 48.4 %gather_rows.1.x_ref = bf16[2048,2048]{1,0:T(8,128)(2,1)} custom-call(bf16[128,2048]{1,0:T(8,128)(2,1)S(1)} %multiply_convert_fusion.x_ref), custom_call_target="tpu_custom_call" | custom-call | tf_op jit(solution)/shard_map/gather_rows/pallas_call | solution.py:258
  128.9 35.0 %experts.1.refs_0_ = bf16[2048,2048]{1,0:T(8,128)(2,1)} custom-call(bf16[2048,2048]{1,0:T(8,128)(2,1)} %gather_rows.1.x_ref, s32[2048,2]{1,0:T(8,128)} %copy.24.rank_ref, s32[8,2048]{1,0:T(8,128)} %pad.13.rank_row_ref, f32[2048,2]{1,0:T(8,128)} %bitcast.33, bf16[2,2048,768]{2,1,0:T(8,128)(2,1)} %gate_hbm.1, bf16[2,2048,768]{2,1,0:T(8,128)(2,1)} %up_hbm.1, ...), custom_call_target="tpu_custom_call" | custom-call | tf_op jit(solution)/shard_map/experts/pallas_call | solution.py:505
  163.9 44.8 %reduce_rows.1 = f32[128,2048]{1,0:T(8,128)S(1)} custom-call(bf16[2048,2048]{1,0:T(8,128)(2,1)} %experts.1.refs_0_), custom_call_target="tpu_custom_call" | custom-call | tf_op jit(solution)/shard_map/reduce_rows/pallas_call | solution.py:411
  208.7 1.0 add_convert_fusion
  (9 shorter events, 0.1 us)
Async XLA Ops:
  0.0 77.4 %copy-start.7 = (f32[2048]{0:T(1024)S(1)}, f32[2048]{0:T(1024)}, u32[]{:S(2)}) copy-start(f32[2048]{0:T(1024)} %param.29) | copy-start | bytes 24580
  4.0 1.2 copy-start
  5.2 1.2 copy-start.1
  6.4 1.2 copy-start.2
  7.6 1.0 copy-start.4
  8.7 1.0 copy-start.5
  9.7 66.5 %copy-start.6 = (bf16[128,2048]{1,0:T(8,128)(2,1)S(1)}, bf16[128,2048]{1,0:T(8,128)(2,1)}, u32[]{:S(2)}) copy-start(bf16[128,2048]{1,0:T(8,128)(2,1)} %param.18) | copy-start | bytes 1572868
  26.2 1.0 copy-start.3
